TPU v7x, 256 devices: a whole 4x4x8 slice. The times are simulated.
256 devices in a mesh: tm: 8 (over y, core), rows: 8 (over z), dp: 4 (over x).
Axes of the slice: x: 4, y: 4, z: 8, core: 2. Of those that a mesh axis runs over, the one named last changes fastest.
Arguments:
- video: bfloat16 [4, 128, 32, 32, 128], P('dp', 'tm', 'rows'), may hold values from -6 to 6
- cotangent: bfloat16 [4, 128, 32, 32, 128], P('dp', 'tm', 'rows'), may hold values from -6 to 6
- in_kernel: bfloat16 [3, 3, 128, 128], replicated, may hold values from -0.03125 to 0.03125
- out_kernel: bfloat16 [3, 3, 128, 128], replicated, may hold values from -0.1875 to 0.1875
- skip_gain: float32 [128], replicated, may hold values from 0.5 to 1.5
- log_decay: float32 [128, 128], P('tm'), may hold values from -3 to 0, as said below
Outputs:
- layer_out: bfloat16 [4, 128, 32, 32, 128], P('dp', 'tm', 'rows')
- video_grad: bfloat16 [4, 128, 32, 32, 128], P('dp', 'tm', 'rows')
- in_kernel_grad: float32 [3, 3, 128, 128], replicated
- out_kernel_grad: float32 [3, 3, 128, 128], replicated
- skip_gain_grad: float32 [128], replicated
- decay_grad: float32 [128, 128], P('tm')
Inputs may be any that keep to these rules, and one draw needn't show every extreme that they name: log_decay is negative.
All inputs are finite; a program needn't handle non-finite values.
Results may differ from a plain program's by a relative error of at most 0.0085.
Values may be sent and summed in bfloat16 or wider, within the bound.
A program may use at most 64 MiB of HBM per device.

v0:
```python
import math
import jax
import jax.numpy as jnp
from jax import lax
from jax.sharding import PartitionSpec as P


def padded_2(cells, sides, width):
    for axis, dim in sides:
        count = lax.axis_size(axis)
        ends = count - 1
        head = lax.slice_in_dim(cells, 0, width, axis=dim)
        tail = lax.slice_in_dim(cells, cells.shape[dim] - width, cells.shape[dim], axis=dim)
        cells = jnp.concatenate(
            [
                lax.ppermute(tail, axis, [(i, (i + 1) % count) for i in range(ends)]),
                cells,
                lax.ppermute(head, axis, [((i + 1) % count, i) for i in range(ends)]),
            ],
            axis=dim,
        )
    return cells


def prefix(value, axis, join, neutral):
    count, mine = (lax.axis_size(axis), lax.axis_index(axis))
    pieces = jax.tree.map(lambda part: lax.all_gather(part, axis), value)
    running = jax.tree.map(
        lambda part, zero: jnp.full_like(part, 0) + jnp.asarray(zero, part.dtype), value, neutral
    )

    def prefix_lap(position, running):
        longer = join(running, jax.tree.map(lambda part: part[position], pieces))
        return jax.tree.map(lambda new, old: jnp.where(position < mine, new, old), longer, running)

    return lax.fori_loop(0, count - 1, prefix_lap, running)


def entering(array, axis, combine, identity):
    devices, position = (lax.axis_size(axis), lax.axis_index(axis))
    everything = jax.tree.map(
        lambda part, kind: lax.all_gather(part.astype(kind), axis),
        array,
        (jnp.bfloat16, jnp.bfloat16),
    )
    start = jax.tree.map(
        lambda part, zero: jnp.broadcast_to(jnp.asarray(zero, part.dtype), part.shape),
        array,
        identity,
    )

    def entering_lap(k, before):
        at = devices - 1 - k
        reached = at > position
        new = combine(
            before, jax.tree.map(lambda part, own: part[at].astype(own.dtype), everything, array)
        )
        return jax.tree.map(lambda a, b: jnp.where(reached, a, b), new, before)

    return lax.fori_loop(0, devices, entering_lap, start)


def pad_columns(field):
    return jnp.pad(field, ((0, 0), (0, 0), (0, 0), (1, 1), (0, 0)))


def forward_conv(padded, kernel):
    seqs, frames, rows_two, cols_two, chans = padded.shape
    rows, cols = (rows_two - 2, cols_two - 2)
    total = None
    for i in range(3):
        for j in range(3):
            piece = padded[:, :, i : i + rows, j : j + cols, :].reshape(-1, chans)
            term = jnp.dot(piece, kernel[i, j], preferred_element_type=jnp.float32)
            total = term if total is None else total + term
    return total.reshape(seqs, frames, rows, cols, kernel.shape[3])


def adjoint_conv(padded, kernel):
    seqs, frames, rows_two, cols_two, chans = padded.shape
    rows, cols = (rows_two - 2, cols_two - 2)
    total = None
    for i in range(3):
        for j in range(3):
            piece = padded[:, :, 2 - i : 2 - i + rows, 2 - j : 2 - j + cols, :].reshape(-1, chans)
            term = lax.dot_general(
                piece, kernel[i, j], (((1,), (1,)), ((), ())), preferred_element_type=jnp.float32
            )
            total = term if total is None else total + term
    return total.reshape(seqs, frames, rows, cols, kernel.shape[2])


def kernel_grad(padded, grad):
    seqs, frames, rows_two, cols_two, chans = padded.shape
    rows, cols = (rows_two - 2, cols_two - 2)
    flat_grad = grad.reshape(-1, grad.shape[-1])
    outer_list = []
    for i in range(3):
        inner_list = []
        for j in range(3):
            piece = padded[:, :, i : i + rows, j : j + cols, :].reshape(-1, chans)
            inner_list.append(
                lax.dot_general(
                    piece, flat_grad, (((0,), (0,)), ((), ())), preferred_element_type=jnp.float32
                )
            )
        outer_list.append(jnp.stack(inner_list))
    return jnp.stack(outer_list)


def combine_groups(earlier, later):
    return (earlier[0] * later[0], later[0] * earlier[1] + later[1])


def on_device(video, cotangent, in_kernel, out_kernel, skip_gain, log_decay):
    seqs, frames, rows, cols, chans = video.shape
    padded_x = pad_columns(padded_2(video, (("rows", 2),), 1))
    drive = forward_conv(padded_x, in_kernel)
    cum = jnp.cumsum(log_decay, axis=0)
    later_mask = (
        lax.broadcasted_iota(jnp.int32, (frames, frames), 0)
        >= lax.broadcasted_iota(jnp.int32, (frames, frames), 1)
    )[:, :, None]
    gaps = cum[:, None, :] - cum[None, :, :]
    within = jnp.where(later_mask, jnp.exp(jnp.where(later_mask, gaps, 0.0)), 0.0)
    local_states = jnp.einsum("tkp,skrcp->strcp", within, drive, precision=lax.Precision.HIGHEST)
    group_total = cum[-1]
    group_decay = jnp.exp(group_total)
    empty = jnp.zeros_like(local_states[:, -1])
    identity = (jnp.ones_like(group_total), empty)
    _, carry_in = prefix((group_decay, local_states[:, -1]), "tm", combine_groups, identity)
    states = local_states + jnp.exp(cum)[None, :, None, None, :] * carry_in[:, None]
    states_bf = states.astype(jnp.bfloat16)
    padded_s = pad_columns(padded_2(states_bf, (("rows", 2),), 1))
    pre = forward_conv(padded_s, out_kernel) + skip_gain * video.astype(jnp.float32)
    activated, pullback = jax.vjp(jax.nn.gelu, pre)
    grad_pre = pullback(cotangent.astype(jnp.float32))[0]
    grad_bf = grad_pre.astype(jnp.bfloat16)
    out_grad = kernel_grad(padded_s, grad_bf)
    gain_grad = jnp.sum(grad_pre * video.astype(jnp.float32), axis=(0, 1, 2, 3))
    padded_g = pad_columns(padded_2(grad_bf, (("rows", 2),), 1))
    state_grad = adjoint_conv(padded_g, out_kernel)
    local_adjoint = jnp.einsum(
        "tkp,strcp->skrcp", within, state_grad, precision=lax.Precision.HIGHEST
    )
    leading = jnp.exp(cum[0])[None, None, None, :] * local_adjoint[:, 0]
    _, back_in = entering((group_decay, leading), "tm", combine_groups, identity)
    adjoint = (
        local_adjoint
        + jnp.exp(group_total[None, :] - cum)[None, :, None, None, :] * back_in[:, None]
    )
    previous = jnp.concatenate([carry_in[:, None], states[:, :-1]], axis=1)
    decay_part = jnp.sum(
        adjoint * jnp.exp(log_decay)[None, :, None, None, :] * previous, axis=(0, 2, 3)
    )
    decay_scale = 1.0 / math.sqrt(seqs * rows * cols * lax.axis_size("rows") * lax.axis_size("dp"))
    decay_grad = lax.psum(decay_part, ("rows", "dp")) * decay_scale
    adjoint_bf = adjoint.astype(jnp.bfloat16)
    in_grad = kernel_grad(padded_x, adjoint_bf)
    padded_a = pad_columns(padded_2(adjoint_bf, (("rows", 2),), 1))
    video_grad = (adjoint_conv(padded_a, in_kernel) + skip_gain * grad_pre).astype(jnp.bfloat16)
    in_sum, out_sum, gain_sum = lax.psum((in_grad, out_grad, gain_grad), ("tm", "rows", "dp"))
    weight_scale = 1.0 / math.sqrt(
        seqs
        * frames
        * rows
        * cols
        * lax.axis_size("tm")
        * lax.axis_size("rows")
        * lax.axis_size("dp")
    )
    return (
        activated.astype(jnp.bfloat16),
        video_grad,
        in_sum * weight_scale,
        out_sum * weight_scale,
        gain_sum * weight_scale,
        decay_grad,
    )


def solution(mesh):
    placed = (
        P("dp", "tm", "rows", None, None),
        P("dp", "tm", "rows", None, None),
        P(),
        P(),
        P(),
        P("tm", None),
    )
    return jax.shard_map(
        on_device,
        mesh=mesh,
        in_specs=placed,
        out_specs=(
            P("dp", "tm", "rows", None, None),
            P("dp", "tm", "rows", None, None),
            P(),
            P(),
            P(),
            P("tm", None),
        ),
        check_vma=False,
    )
```

profile of v0, /device:TPU:8, one launch (start us, length us, event | category | flops | bytes accessed | tf_op | source)
XLA Modules:
  0.0 646.0 jit_solution(3192037692985163156)
XLA Ops:
  8.2 3.8 collective-permute-start
  14.8 8.7 %all-gather = f32[8,1,128]{2,1,0:T(1,128)S(1)} all-gather(f32[1,1,128]{2,1,0:T(1,128)S(1)} %get-tuple-element.381), channel_id=1, replica_groups=mesh['tm'=8,'rows'=8,'dp'=4] {'tm'}, dimensions={0}, use_global_device_ids=true | all-gather | bytes 4608 | tf_op jit(solution)/shard_map/all_gather | solution.py:27
  23.5 1.6 fusion.27
  29.1 4.5 copy.179
  33.6 8.3 %fusion.21 = f32[128,4,32,16]{2,3,1,0:T(8,128)} fusion(f32[16,4,32,128]{2,0,1,3:T(8,128)} %copy.179, f32[16,128]{0,1:T(8,128)S(1)} %copy.177, pred[16,16]{0,1:T(8,128)(4,1)S(1)} %iota_compare_fusion.2), kind=kOutput, calls=%fused_computation.80 | convolution fusion | flops 50429952 | bytes 2105600 | tf_op jit(solution)/shard_map/tkp,skrcp->strcp/dot_general | solution.py:126
  41.9 3.7 copy.181
  45.6 12.7 %all_gather.16 = f32[8,1,4,32,128]{4,3,2,1,0:T(8,128)S(1)} all-gather(f32[1,1,4,32,128]{4,3,2,1,0:T(8,128)S(1)} %slice.319), channel_id=1, replica_groups=mesh['tm'=8,'rows'=8,'dp'=4] {'tm'}, dimensions={0}, use_global_device_ids=true | all-gather | bytes 589824 | tf_op jit(solution)/shard_map/all_gather | solution.py:27
  58.7 2.4 fusion.171
  61.2 4.6 collective-permute-start.2
  67.1 11.1 %all-gather.1 = bf16[8,1,128]{2,1,0:T(2,128)(2,1)S(1)} all-gather(bf16[1,1,128]{2,1,0:T(2,128)(2,1)S(1)} %get-tuple-element.380), channel_id=1, replica_groups=mesh['tm'=8,'rows'=8,'dp'=4] {'tm'}, dimensions={0}, use_global_device_ids=true | all-gather | bytes 2304 | tf_op jit(solution)/shard_map/all_gather | solution.py:42
  78.8 2.3 slice.346
  85.9 2.3 fusion.8
  97.1 4.6 collective-permute-start.4
  103.0 80.3 %psum.30 = f32[128]{0:T(128)S(1)} all-reduce(f32[128]{0:T(128)S(1)} %copy-done.25), channel_id=1, replica_groups=mesh['tm'=8,'rows'=8,'dp'=4] {'tm','rows','dp'}, use_global_device_ids=true, to_apply=%region_8.9 | all-reduce | flops 128 | bytes 1024 | tf_op jit(solution)/shard_map/psum | solution.py:162
  189.9 4.5 copy.182
  194.4 8.2 %fusion.19 = f32[128,4,32,16]{2,3,1,0:T(8,128)} fusion(f32[16,4,32,128]{2,0,1,3:T(8,128)} %copy.182, f32[16,128]{0,1:T(8,128)S(1)} %copy.177, pred[16,16]{0,1:T(8,128)(4,1)S(1)} %copy-done.21), kind=kOutput, calls=%fused_computation.78 | convolution fusion | flops 50429952 | bytes 2105600 | tf_op jit(solution)/shard_map/tkp,strcp->skrcp/dot_general | solution.py:143
  202.6 3.7 copy.183
  206.3 13.1 %all_gather.18 = bf16[8,1,4,32,128]{4,3,2,1,0:T(8,128)(2,1)S(1)} all-gather(bf16[1,1,4,32,128]{4,3,2,1,0:T(8,128)(2,1)S(1)} %fusion.73), channel_id=1, replica_groups=mesh['tm'=8,'rows'=8,'dp'=4] {'tm'}, dimensions={0}, use_global_device_ids=true | all-gather | bytes 294912 | tf_op jit(solution)/shard_map/all_gather | solution.py:42
  219.4 5.9 while.31
  230.4 3.7 collective-permute-start.6
  235.4 141.5 %psum.31 = f32[16,128]{0,1:T(8,128)S(1)} all-reduce(f32[16,128]{0,1:T(8,128)S(1)} %copy.211), channel_id=1, replica_groups=mesh['tm'=8,'rows'=8,'dp'=4] {'rows','dp'}, use_global_device_ids=true, to_apply=%region_10.11 | all-reduce | flops 2048 | bytes 16384 | tf_op jit(solution)/shard_map/psum | solution.py:157
  384.8 250.3 %all-reduce.7.cloned.1.call-done = (f32[3,3,128,128]{3,2,1,0:T(8,128)}, f32[3,3,128,128]{3,2,1,0:T(8,128)}) async-done(((f32[3,3,128,128]{3,2,1,0:T(8,128)}, f32[3,3,128,128]{3,2,1,0:T(8,128)}), (f32[3,3,128,128]{3,2,1,0:T(8,128)}, f32[3,3,128,128]{3,2,1,0:T(8,128)})) %all-reduce.7.cloned.1.call-update) | async-done | bytes 1179664 | tf_op jit(solution)/shard_map/psum | solution.py:162
  635.1 1.9 broadcast_multiply_fusion
  637.0 1.9 broadcast_multiply_fusion.1
  (190 shorter events, 51.3 us)
Async XLA Ops:
  7.2 627.9 %all-reduce.7.cloned.1.call-start = ((), (), s32[]{:S(2)}) async-start(), calls=%async_computation | async-start | bytes 2359296 | tf_op jit(solution)/shard_map/psum | solution.py:162
  8.2 15.3 %collective-permute-start = (bf16[1,16,1,32,128]{4,3,2,1,0:T(8,128)(2,1)S(1)}, bf16[1,16,1,32,128]{4,3,2,1,0:T(8,128)(2,1)S(1)}, u32[]{:S(2)}, u32[]{:S(2)}) collective-permute-start(bf16[1,16,1,32,128]{4,3,2,1,0:T(8,128)(2,1)S(1)} %get-tuple-element.375), channel_id=1, source_target_pairs={{0,4},{4,8},{8,12},{12,16},{16,20},{20,24},{24,28},{1,5},{5,9},{9,... | collective-permute-start | bytes 393224 | tf_op jit(solution)/shard_map/ppermute | solution.py:16
  12.0 11.5 %collective-permute-start.1 = (bf16[1,16,1,32,128]{4,3,2,1,0:T(8,128)(2,1)S(1)}, bf16[1,16,1,32,128]{4,3,2,1,0:T(8,128)(2,1)S(1)}, u32[]{:S(2)}, u32[]{:S(2)}) collective-permute-start(bf16[1,16,1,32,128]{4,3,2,1,0:T(8,128)(2,1)S(1)} %get-tuple-element.376), channel_id=1, source_target_pairs={{4,0},{8,4},{12,8},{16,12},{20,16},{24,20},{28,24},{5,1},{9,5},{13... | collective-permute-start | bytes 393224 | tf_op jit(solution)/shard_map/ppermute | solution.py:18
  23.5 10.1 %copy-start.20 = (pred[16,16]{0,1:T(8,128)(4,1)}, pred[16,16]{0,1:T(8,128)(4,1)S(1)}, u32[]{:S(2)}) copy-start(pred[16,16]{0,1:T(8,128)(4,1)S(1)} %iota_compare_fusion.2) | copy-start | bytes 772
  26.9 1.9 copy-start.4
  45.6 13.1 %copy-start.3 = (f32[128,4,32,16]{0,2,1,3:T(8,128)}, f32[128,4,32,16]{0,2,1,3:T(8,128)S(1)}, u32[]{:S(2)}) copy-start(f32[128,4,32,16]{0,2,1,3:T(8,128)S(1)} %copy.181) | copy-start | bytes 3145732
  58.3 8.7 %copy-start.19 = (f32[16,128]{1,0:T(8,128)S(1)}, f32[16,128]{1,0:T(8,128)}, u32[]{:S(2)}) copy-start(f32[16,128]{1,0:T(8,128)} %param.15) | copy-start | bytes 24580
  61.2 19.9 %collective-permute-start.2 = (bf16[1,16,1,32,128]{4,3,2,1,0:T(8,128)(2,1)S(1)}, bf16[1,16,1,32,128]{4,3,2,1,0:T(8,128)(2,1)S(1)}, u32[]{:S(2)}, u32[]{:S(2)}) collective-permute-start(bf16[1,16,1,32,128]{4,3,2,1,0:T(8,128)(2,1)S(1)} %get-tuple-element.371), channel_id=1, source_target_pairs={{0,4},{4,8},{8,12},{12,16},{16,20},{20,24},{24,28},{1,5},{5,9},{9,... | collective-permute-start | bytes 393224 | tf_op jit(solution)/shard_map/ppermute | solution.py:16
  65.7 15.3 %collective-permute-start.3 = (bf16[1,16,1,32,128]{4,3,2,1,0:T(8,128)(2,1)S(1)}, bf16[1,16,1,32,128]{4,3,2,1,0:T(8,128)(2,1)S(1)}, u32[]{:S(2)}, u32[]{:S(2)}) collective-permute-start(bf16[1,16,1,32,128]{4,3,2,1,0:T(8,128)(2,1)S(1)} %get-tuple-element.372), channel_id=1, source_target_pairs={{4,0},{8,4},{12,8},{16,12},{20,16},{24,20},{28,24},{5,1},{9,5},{13... | collective-permute-start | bytes 393224 | tf_op jit(solution)/shard_map/ppermute | solution.py:18
  88.2 2.0 copy-start.1
  95.1 7.9 %copy-start.25 = (f32[128]{0:T(128)S(1)}, f32[128]{0:T(128)}, u32[]{:S(2)}) copy-start(f32[128]{0:T(128)} %get-tuple-element.330) | copy-start | bytes 1540
  95.1 88.7 %copy-start.13 = (f32[1,128,128]{2,1,0:T(8,128)S(1)}, f32[1,128,128]{2,1,0:T(8,128)}, u32[]{:S(2)}) copy-start(f32[1,128,128]{2,1,0:T(8,128)} %convolution_bitcast_fusion.7) | copy-start | bytes 196612
  95.1 88.7 %copy-start.14 = (f32[1,128,128]{2,1,0:T(8,128)S(1)}, f32[1,128,128]{2,1,0:T(8,128)}, u32[]{:S(2)}) copy-start(f32[1,128,128]{2,1,0:T(8,128)} %convolution_bitcast_fusion.3) | copy-start | bytes 196612
  95.1 88.7 %copy-start.15 = (f32[1,128,128]{2,1,0:T(8,128)S(1)}, f32[1,128,128]{2,1,0:T(8,128)}, u32[]{:S(2)}) copy-start(f32[1,128,128]{2,1,0:T(8,128)} %convolution_bitcast_fusion.5) | copy-start | bytes 196612
  95.1 88.7 %copy-start.16 = (f32[1,128,128]{2,1,0:T(8,128)S(1)}, f32[1,128,128]{2,1,0:T(8,128)}, u32[]{:S(2)}) copy-start(f32[1,128,128]{2,1,0:T(8,128)} %convolution_bitcast_fusion.6) | copy-start | bytes 196612
  95.1 88.7 %copy-start.17 = (f32[1,128,128]{2,1,0:T(8,128)S(1)}, f32[1,128,128]{2,1,0:T(8,128)}, u32[]{:S(2)}) copy-start(f32[1,128,128]{2,1,0:T(8,128)} %convolution_bitcast_fusion.8) | copy-start | bytes 196612
  95.1 88.7 %copy-start.18 = (f32[1,128,128]{2,1,0:T(8,128)S(1)}, f32[1,128,128]{2,1,0:T(8,128)}, u32[]{:S(2)}) copy-start(f32[1,128,128]{2,1,0:T(8,128)} %convolution_bitcast_fusion.4) | copy-start | bytes 196612
  97.1 88.5 %collective-permute-start.4 = (bf16[1,16,1,32,128]{4,3,2,1,0:T(8,128)(2,1)S(1)}, bf16[1,16,1,32,128]{4,3,2,1,0:T(8,128)(2,1)S(1)}, u32[]{:S(2)}, u32[]{:S(2)}) collective-permute-start(bf16[1,16,1,32,128]{4,3,2,1,0:T(8,128)(2,1)S(1)} %get-tuple-element.367), channel_id=1, source_target_pairs={{0,4},{4,8},{8,12},{12,16},{16,20},{20,24},{24,28},{1,5},{5,9},{9,... | collective-permute-start | bytes 393224 | tf_op jit(solution)/shard_map/ppermute | solution.py:16
  101.7 84.0 %collective-permute-start.5 = (bf16[1,16,1,32,128]{4,3,2,1,0:T(8,128)(2,1)S(1)}, bf16[1,16,1,32,128]{4,3,2,1,0:T(8,128)(2,1)S(1)}, u32[]{:S(2)}, u32[]{:S(2)}) collective-permute-start(bf16[1,16,1,32,128]{4,3,2,1,0:T(8,128)(2,1)S(1)} %get-tuple-element.368), channel_id=1, source_target_pairs={{4,0},{8,4},{12,8},{16,12},{20,16},{24,20},{28,24},{5,1},{9,5},{13... | collective-permute-start | bytes 393224 | tf_op jit(solution)/shard_map/ppermute | solution.py:18
  189.9 4.5 copy-start.21
  202.6 3.7 copy-start.22
  230.4 148.2 %collective-permute-start.6 = (bf16[1,16,1,32,128]{4,3,2,1,0:T(8,128)(2,1)S(1)}, bf16[1,16,1,32,128]{4,3,2,1,0:T(8,128)(2,1)S(1)}, u32[]{:S(2)}, u32[]{:S(2)}) collective-permute-start(bf16[1,16,1,32,128]{4,3,2,1,0:T(8,128)(2,1)S(1)} %get-tuple-element.363), channel_id=1, source_target_pairs={{0,4},{4,8},{8,12},{12,16},{16,20},{20,24},{24,28},{1,5},{5,9},{9,... | collective-permute-start | bytes 393224 | tf_op jit(solution)/shard_map/ppermute | solution.py:16
  234.0 144.5 %collective-permute-start.7 = (bf16[1,16,1,32,128]{4,3,2,1,0:T(8,128)(2,1)S(1)}, bf16[1,16,1,32,128]{4,3,2,1,0:T(8,128)(2,1)S(1)}, u32[]{:S(2)}, u32[]{:S(2)}) collective-permute-start(bf16[1,16,1,32,128]{4,3,2,1,0:T(8,128)(2,1)S(1)} %get-tuple-element.364), channel_id=1, source_target_pairs={{4,0},{8,4},{12,8},{16,12},{20,16},{24,20},{28,24},{5,1},{9,5},{13... | collective-permute-start | bytes 393224 | tf_op jit(solution)/shard_map/ppermute | solution.py:18
  382.5 1.2 copy-start.2
  (11 other events, 11.1 us)
Sparse Core Ops, SparseCore 0:
  378.7 256.3 all-reduce.6
where the time goes:
time: 655 us; the launch traced here: 646 us
  blocking collectives  267 us (41%)
  waiting for transfers between devices  250 us (38%)
  matrix products  38.6 us (6%)
  local copies, waits for them, and re-layouts  27.4 us (4%)
  other arithmetic  25 us (4%)
  starting transfers between devices  21.8 us (3%)
  between operations  15 us (2%)
    psum x1, waiting for transfers between devices, on_device(): lax.psum((in_grad, out_grad, gain_grad), ('tm', 'rows', 'dp'))  250 us
    psum x1, blocking collectives, on_device(): decay_grad = lax.psum(decay_part, ('rows', 'dp')) * decay_scale  142 us
    psum x1, blocking collectives, on_device(): lax.psum((in_grad, out_grad, gain_grad), ('tm', 'rows', 'dp'))  80.3 us
    all_gather x2, blocking collectives, entering(): lax.all_gather(part.astype(kind), axis)  24.3 us
    all_gather x2, blocking collectives, prefix(): pieces = jax.tree.map(lambda part: lax.all_gather(part, axis), value)  21.4 us
    ppermute x4, starting transfers between devices, padded_2(): lax.ppermute(tail, axis, [(i, (i + 1) % count) for i in range(ends)])  16.6 us
  transfers between devices with their start and end apart: 9, of which 1 were waited for; matrix products, arithmetic and copies ran while one was open for 2% of the time, Pallas kernels for 0%

commit v1 on v0

--- a/solution.py
+++ b/solution.py
@@ -154,7 +154,7 @@
         adjoint * jnp.exp(log_decay)[None, :, None, None, :] * previous, axis=(0, 2, 3)
     )
     decay_scale = 1.0 / math.sqrt(seqs * rows * cols * lax.axis_size("rows") * lax.axis_size("dp"))
-    decay_grad = lax.psum(decay_part, ("rows", "dp")) * decay_scale
+    decay_grad = lax.psum(lax.psum(decay_part, "rows"), "dp") * decay_scale
     adjoint_bf = adjoint.astype(jnp.bfloat16)
     in_grad = kernel_grad(padded_x, adjoint_bf)
     padded_a = pad_columns(padded_2(adjoint_bf, (("rows", 2),), 1))

time: 655 us -> 561 us (0.86)
  blocking collectives: 267 us -> 173 us
    psum x1 -> x2, blocking collectives: 142 us -> 46.6 us  [on_device(): decay_grad = lax.psum(lax.psum(decay_part, 'rows'), 'dp') * decay_scale]
where the time goes in v1:
time: 561 us; the launch traced here: 552 us
  waiting for transfers between devices  251 us (45%)
  blocking collectives  173 us (31%)
  matrix products  38.5 us (7%)
  local copies, waits for them, and re-layouts  27.4 us (5%)
  other arithmetic  24.9 us (4%)
  starting transfers between devices  21.8 us (4%)
  between operations  15 us (3%)
    psum x1, waiting for transfers between devices, on_device(): lax.psum((in_grad, out_grad, gain_grad), ('tm', 'rows', 'dp'))  251 us
    psum x1, blocking collectives, on_device(): lax.psum((in_grad, out_grad, gain_grad), ('tm', 'rows', 'dp'))  80.3 us
    psum x2, blocking collectives, on_device(): decay_grad = lax.psum(lax.psum(decay_part, 'rows'), 'dp') * decay_scale  46.6 us
    all_gather x2, blocking collectives, entering(): lax.all_gather(part.astype(kind), axis)  24.3 us
    all_gather x2, blocking collectives, prefix(): pieces = jax.tree.map(lambda part: lax.all_gather(part, axis), value)  21.4 us
    ppermute x4, starting transfers between devices, padded_2(): lax.ppermute(tail, axis, [(i, (i + 1) % count) for i in range(ends)])  16.6 us
    dot_general x18, matrix products, kernel_grad(): lax.dot_general(piece, flat_grad, (((0,), (0,)), ((), ())), preferred_ele...  11.7 us
  transfers between devices with their start and end apart: 9, of which 1 were waited for; matrix products, arithmetic and copies ran while one was open for 2% of the time, Pallas kernels for 0%

profile of v1, /device:TPU:8, one launch (start us, length us, event | category | flops | bytes accessed | tf_op | source)
XLA Modules:
  0.0 551.8 jit_solution(13605099137912416305)
XLA Ops:
  8.2 3.8 collective-permute-start
  14.7 8.7 %all-gather = f32[8,1,128]{2,1,0:T(1,128)S(1)} all-gather(f32[1,1,128]{2,1,0:T(1,128)S(1)} %get-tuple-element.381), channel_id=1, replica_groups=mesh['tm'=8,'rows'=8,'dp'=4] {'tm'}, dimensions={0}, use_global_device_ids=true | all-gather | bytes 4608 | tf_op jit(solution)/shard_map/all_gather | solution.py:27
  29.0 4.5 copy.179
  33.5 8.3 %fusion.21 = f32[128,4,32,16]{2,3,1,0:T(8,128)} fusion(f32[16,4,32,128]{2,0,1,3:T(8,128)} %copy.179, f32[16,128]{0,1:T(8,128)S(1)} %copy.177, pred[16,16]{0,1:T(8,128)(4,1)S(1)} %iota_compare_fusion.2), kind=kOutput, calls=%fused_computation.80 | convolution fusion | flops 50429952 | bytes 2105600 | tf_op jit(solution)/shard_map/tkp,skrcp->strcp/dot_general | solution.py:126
  41.8 3.7 copy.181
  45.6 12.7 %all_gather.16 = f32[8,1,4,32,128]{4,3,2,1,0:T(8,128)S(1)} all-gather(f32[1,1,4,32,128]{4,3,2,1,0:T(8,128)S(1)} %slice.319), channel_id=1, replica_groups=mesh['tm'=8,'rows'=8,'dp'=4] {'tm'}, dimensions={0}, use_global_device_ids=true | all-gather | bytes 589824 | tf_op jit(solution)/shard_map/all_gather | solution.py:27
  58.7 2.4 fusion.171
  61.1 4.6 collective-permute-start.2
  67.0 11.1 %all-gather.1 = bf16[8,1,128]{2,1,0:T(2,128)(2,1)S(1)} all-gather(bf16[1,1,128]{2,1,0:T(2,128)(2,1)S(1)} %get-tuple-element.380), channel_id=1, replica_groups=mesh['tm'=8,'rows'=8,'dp'=4] {'tm'}, dimensions={0}, use_global_device_ids=true | all-gather | bytes 2304 | tf_op jit(solution)/shard_map/all_gather | solution.py:42
  78.7 2.2 slice.346
  85.9 2.3 fusion.8
  97.0 4.5 collective-permute-start.4
  102.9 80.3 %psum.37 = f32[128]{0:T(128)S(1)} all-reduce(f32[128]{0:T(128)S(1)} %copy-done.25), channel_id=1, replica_groups=mesh['tm'=8,'rows'=8,'dp'=4] {'tm','rows','dp'}, use_global_device_ids=true, to_apply=%region_8.9 | all-reduce | flops 128 | bytes 1024 | tf_op jit(solution)/shard_map/psum | solution.py:162
  189.8 4.5 copy.182
  194.3 8.2 %fusion.19 = f32[128,4,32,16]{2,3,1,0:T(8,128)} fusion(f32[16,4,32,128]{2,0,1,3:T(8,128)} %copy.182, f32[16,128]{0,1:T(8,128)S(1)} %copy.177, pred[16,16]{0,1:T(8,128)(4,1)S(1)} %copy-done.21), kind=kOutput, calls=%fused_computation.78 | convolution fusion | flops 50429952 | bytes 2105600 | tf_op jit(solution)/shard_map/tkp,strcp->skrcp/dot_general | solution.py:143
  202.5 3.7 copy.183
  206.2 13.1 %all_gather.18 = bf16[8,1,4,32,128]{4,3,2,1,0:T(8,128)(2,1)S(1)} all-gather(bf16[1,1,4,32,128]{4,3,2,1,0:T(8,128)(2,1)S(1)} %fusion.73), channel_id=1, replica_groups=mesh['tm'=8,'rows'=8,'dp'=4] {'tm'}, dimensions={0}, use_global_device_ids=true | all-gather | bytes 294912 | tf_op jit(solution)/shard_map/all_gather | solution.py:42
  219.3 5.9 %while.31 = (s32[]{:T(128)}, f32[1,4,32,128]{3,2,1,0:T(8,128)S(1)}, s32[]{:T(128)}, bf16[8,128]{1,0:T(8,128)(2,1)}, bf16[8,1,4,32,128]{4,3,2,1,0:T(8,128)(2,1)S(...) while((s32[]{:T(128)}, f32[1,4,32,128]{3,2,1,0:T(8,128)S(1)}, s32[]{:T(128)}, ...), condition=%wide.region_4.5_spmd.clone, body=%wide.region_3.4_spmd.clone.sunk | while | flops 82056 | bytes 165287 | solution.py:60
  230.3 3.6 collective-permute-start.6
  235.3 31.2 %psum.38 = f32[16,128]{0,1:T(8,128)S(1)} all-reduce(f32[16,128]{0,1:T(8,128)S(1)} %copy.211), channel_id=1, replica_groups=mesh['tm'=8,'rows'=8,'dp'=4] {'rows'}, use_global_device_ids=true, to_apply=%region_10.11 | all-reduce | flops 2048 | bytes 16384 | tf_op jit(solution)/shard_map/psum | solution.py:157
  266.5 15.4 %psum.39 = f32[16,128]{0,1:T(8,128)S(1)} all-reduce(f32[16,128]{0,1:T(8,128)S(1)} %psum.38), channel_id=1, replica_groups=mesh['tm'=8,'rows'=8,'dp'=4] {'dp'}, use_global_device_ids=true, to_apply=%region_11.12 | all-reduce | flops 2048 | bytes 16384 | tf_op jit(solution)/shard_map/psum | solution.py:157
  289.8 251.1 %all-reduce.7.cloned.1.call-done = (f32[3,3,128,128]{3,2,1,0:T(8,128)}, f32[3,3,128,128]{3,2,1,0:T(8,128)}) async-done(((f32[3,3,128,128]{3,2,1,0:T(8,128)}, f32[3,3,128,128]{3,2,1,0:T(8,128)}), (f32[3,3,128,128]{3,2,1,0:T(8,128)}, f32[3,3,128,128]{3,2,1,0:T(8,128)})) %all-reduce.7.cloned.1.call-update) | async-done | bytes 1179664 | tf_op jit(solution)/shard_map/psum | solution.py:162
  540.9 1.9 broadcast_multiply_fusion
  542.8 1.9 broadcast_multiply_fusion.1
  (191 shorter events, 52.8 us)
Async XLA Ops:
  7.2 533.7 %all-reduce.7.cloned.1.call-start = ((), (), s32[]{:S(2)}) async-start(), calls=%async_computation | async-start | bytes 2359296 | tf_op jit(solution)/shard_map/psum | solution.py:162
  8.2 15.2 %collective-permute-start = (bf16[1,16,1,32,128]{4,3,2,1,0:T(8,128)(2,1)S(1)}, bf16[1,16,1,32,128]{4,3,2,1,0:T(8,128)(2,1)S(1)}, u32[]{:S(2)}, u32[]{:S(2)}) collective-permute-start(bf16[1,16,1,32,128]{4,3,2,1,0:T(8,128)(2,1)S(1)} %get-tuple-element.375), channel_id=1, source_target_pairs={{0,4},{4,8},{8,12},{12,16},{16,20},{20,24},{24,28},{1,5},{5,9},{9,... | collective-permute-start | bytes 393224 | tf_op jit(solution)/shard_map/ppermute | solution.py:16
  12.0 11.4 %collective-permute-start.1 = (bf16[1,16,1,32,128]{4,3,2,1,0:T(8,128)(2,1)S(1)}, bf16[1,16,1,32,128]{4,3,2,1,0:T(8,128)(2,1)S(1)}, u32[]{:S(2)}, u32[]{:S(2)}) collective-permute-start(bf16[1,16,1,32,128]{4,3,2,1,0:T(8,128)(2,1)S(1)} %get-tuple-element.376), channel_id=1, source_target_pairs={{4,0},{8,4},{12,8},{16,12},{20,16},{24,20},{28,24},{5,1},{9,5},{13... | collective-permute-start | bytes 393224 | tf_op jit(solution)/shard_map/ppermute | solution.py:18
  23.4 10.1 %copy-start.20 = (pred[16,16]{0,1:T(8,128)(4,1)}, pred[16,16]{0,1:T(8,128)(4,1)S(1)}, u32[]{:S(2)}) copy-start(pred[16,16]{0,1:T(8,128)(4,1)S(1)} %iota_compare_fusion.2) | copy-start | bytes 772
  26.8 1.9 copy-start.4
  45.6 13.1 %copy-start.3 = (f32[128,4,32,16]{0,2,1,3:T(8,128)}, f32[128,4,32,16]{0,2,1,3:T(8,128)S(1)}, u32[]{:S(2)}) copy-start(f32[128,4,32,16]{0,2,1,3:T(8,128)S(1)} %copy.181) | copy-start | bytes 3145732
  58.3 8.7 %copy-start.19 = (f32[16,128]{1,0:T(8,128)S(1)}, f32[16,128]{1,0:T(8,128)}, u32[]{:S(2)}) copy-start(f32[16,128]{1,0:T(8,128)} %param.15) | copy-start | bytes 24580
  61.1 19.9 %collective-permute-start.2 = (bf16[1,16,1,32,128]{4,3,2,1,0:T(8,128)(2,1)S(1)}, bf16[1,16,1,32,128]{4,3,2,1,0:T(8,128)(2,1)S(1)}, u32[]{:S(2)}, u32[]{:S(2)}) collective-permute-start(bf16[1,16,1,32,128]{4,3,2,1,0:T(8,128)(2,1)S(1)} %get-tuple-element.371), channel_id=1, source_target_pairs={{0,4},{4,8},{8,12},{12,16},{16,20},{20,24},{24,28},{1,5},{5,9},{9,... | collective-permute-start | bytes 393224 | tf_op jit(solution)/shard_map/ppermute | solution.py:16
  65.7 15.3 %collective-permute-start.3 = (bf16[1,16,1,32,128]{4,3,2,1,0:T(8,128)(2,1)S(1)}, bf16[1,16,1,32,128]{4,3,2,1,0:T(8,128)(2,1)S(1)}, u32[]{:S(2)}, u32[]{:S(2)}) collective-permute-start(bf16[1,16,1,32,128]{4,3,2,1,0:T(8,128)(2,1)S(1)} %get-tuple-element.372), channel_id=1, source_target_pairs={{4,0},{8,4},{12,8},{16,12},{20,16},{24,20},{28,24},{5,1},{9,5},{13... | collective-permute-start | bytes 393224 | tf_op jit(solution)/shard_map/ppermute | solution.py:18
  88.1 2.1 copy-start.1
  95.0 7.9 %copy-start.25 = (f32[128]{0:T(128)S(1)}, f32[128]{0:T(128)}, u32[]{:S(2)}) copy-start(f32[128]{0:T(128)} %get-tuple-element.330) | copy-start | bytes 1540
  95.0 88.7 %copy-start.13 = (f32[1,128,128]{2,1,0:T(8,128)S(1)}, f32[1,128,128]{2,1,0:T(8,128)}, u32[]{:S(2)}) copy-start(f32[1,128,128]{2,1,0:T(8,128)} %convolution_bitcast_fusion.7) | copy-start | bytes 196612
  95.0 88.7 %copy-start.14 = (f32[1,128,128]{2,1,0:T(8,128)S(1)}, f32[1,128,128]{2,1,0:T(8,128)}, u32[]{:S(2)}) copy-start(f32[1,128,128]{2,1,0:T(8,128)} %convolution_bitcast_fusion.3) | copy-start | bytes 196612
  95.0 88.7 %copy-start.15 = (f32[1,128,128]{2,1,0:T(8,128)S(1)}, f32[1,128,128]{2,1,0:T(8,128)}, u32[]{:S(2)}) copy-start(f32[1,128,128]{2,1,0:T(8,128)} %convolution_bitcast_fusion.5) | copy-start | bytes 196612
  95.0 88.7 %copy-start.16 = (f32[1,128,128]{2,1,0:T(8,128)S(1)}, f32[1,128,128]{2,1,0:T(8,128)}, u32[]{:S(2)}) copy-start(f32[1,128,128]{2,1,0:T(8,128)} %convolution_bitcast_fusion.6) | copy-start | bytes 196612
  95.0 88.7 %copy-start.17 = (f32[1,128,128]{2,1,0:T(8,128)S(1)}, f32[1,128,128]{2,1,0:T(8,128)}, u32[]{:S(2)}) copy-start(f32[1,128,128]{2,1,0:T(8,128)} %convolution_bitcast_fusion.8) | copy-start | bytes 196612
  95.0 88.7 %copy-start.18 = (f32[1,128,128]{2,1,0:T(8,128)S(1)}, f32[1,128,128]{2,1,0:T(8,128)}, u32[]{:S(2)}) copy-start(f32[1,128,128]{2,1,0:T(8,128)} %convolution_bitcast_fusion.4) | copy-start | bytes 196612
  97.0 88.5 %collective-permute-start.4 = (bf16[1,16,1,32,128]{4,3,2,1,0:T(8,128)(2,1)S(1)}, bf16[1,16,1,32,128]{4,3,2,1,0:T(8,128)(2,1)S(1)}, u32[]{:S(2)}, u32[]{:S(2)}) collective-permute-start(bf16[1,16,1,32,128]{4,3,2,1,0:T(8,128)(2,1)S(1)} %get-tuple-element.367), channel_id=1, source_target_pairs={{0,4},{4,8},{8,12},{12,16},{16,20},{20,24},{24,28},{1,5},{5,9},{9,... | collective-permute-start | bytes 393224 | tf_op jit(solution)/shard_map/ppermute | solution.py:16
  101.6 84.0 %collective-permute-start.5 = (bf16[1,16,1,32,128]{4,3,2,1,0:T(8,128)(2,1)S(1)}, bf16[1,16,1,32,128]{4,3,2,1,0:T(8,128)(2,1)S(1)}, u32[]{:S(2)}, u32[]{:S(2)}) collective-permute-start(bf16[1,16,1,32,128]{4,3,2,1,0:T(8,128)(2,1)S(1)} %get-tuple-element.368), channel_id=1, source_target_pairs={{4,0},{8,4},{12,8},{16,12},{20,16},{24,20},{28,24},{5,1},{9,5},{13... | collective-permute-start | bytes 393224 | tf_op jit(solution)/shard_map/ppermute | solution.py:18
  189.8 4.5 copy-start.21
  202.5 3.7 copy-start.22
  230.3 53.3 %collective-permute-start.6 = (bf16[1,16,1,32,128]{4,3,2,1,0:T(8,128)(2,1)S(1)}, bf16[1,16,1,32,128]{4,3,2,1,0:T(8,128)(2,1)S(1)}, u32[]{:S(2)}, u32[]{:S(2)}) collective-permute-start(bf16[1,16,1,32,128]{4,3,2,1,0:T(8,128)(2,1)S(1)} %get-tuple-element.363), channel_id=1, source_target_pairs={{0,4},{4,8},{8,12},{12,16},{16,20},{20,24},{24,28},{1,5},{5,9},{9,... | collective-permute-start | bytes 393224 | tf_op jit(solution)/shard_map/ppermute | solution.py:16
  233.9 49.6 %collective-permute-start.7 = (bf16[1,16,1,32,128]{4,3,2,1,0:T(8,128)(2,1)S(1)}, bf16[1,16,1,32,128]{4,3,2,1,0:T(8,128)(2,1)S(1)}, u32[]{:S(2)}, u32[]{:S(2)}) collective-permute-start(bf16[1,16,1,32,128]{4,3,2,1,0:T(8,128)(2,1)S(1)} %get-tuple-element.364), channel_id=1, source_target_pairs={{4,0},{8,4},{12,8},{16,12},{20,16},{24,20},{28,24},{5,1},{9,5},{13... | collective-permute-start | bytes 393224 | tf_op jit(solution)/shard_map/ppermute | solution.py:18
  287.5 1.2 copy-start.2
  (11 other events, 11.1 us)
Sparse Core Ops, SparseCore 0:
  283.7 257.1 all-reduce.6
